TPU v7x, 256 devices: a whole 4x4x8 slice. The times are simulated.
256 devices in a mesh: batch: 16 (over z, core), tensor: 16 (over y, x).
Axes of the slice: x: 4, y: 4, z: 8, core: 2. Of those that a mesh axis runs over, the one named last changes fastest.
Arguments:
- inputs: bfloat16 [3, 256, 8192], P(None, None, 'batch'), may hold values from -40 to 40
- in_gain: float32 [8192], P('batch'), may hold values from 0.1 to 1.9
- qkv_weight: bfloat16 [8192, 24576], P('batch', 'tensor'), may hold values from -0.0625 to 0.0625
- decay: float32 [64], P('tensor'), may hold values from 0.25 to 0.99
- state: float32 [256, 64, 128, 128], P('batch', 'tensor'), may hold values from -1.8 to 1.8
- head_gain: float32 [8192], P('tensor'), may hold values from 0.1 to 1.9
- out_weight: bfloat16 [8192, 8192], P('tensor', 'batch'), may hold values from -0.0625 to 0.0625
- mid_gain: float32 [8192], P('batch'), may hold values from 0.1 to 1.9
- up_weight: bfloat16 [8192, 28672], P('batch', 'tensor'), may hold values from -0.0625 to 0.0625
- down_weight: bfloat16 [28672, 8192], P('tensor', 'batch'), may hold values from -0.03125 to 0.03125
- att_mask: int32 [3, 256, 8192], P(None, 'batch', 'tensor'), may hold values 0 or 1
- ffn_mask: int32 [3, 256, 28672], P(None, 'batch', 'tensor'), may hold values 0 or 1
Outputs:
- outputs: bfloat16 [3, 256, 8192], P(None, 'tensor', 'batch')
All inputs are finite; a program needn't handle non-finite values. No bound on the sum of `att_mask` or of `ffn_mask` on one device may be relied on, other than what follows from the above.
Results may differ from a plain program's by a relative error of at most 0.0038.
Values may be sent and summed in bfloat16 or wider, within the bound.
No kernel may reach another device: no remote copies, remote signals or barrier semaphores. Data moves between devices by JAX's collectives and lax.ppermute only.
A program may use at most 64 MiB of HBM per device.

v0:
```python
import jax
import jax.numpy as jnp
from jax import lax
from jax.sharding import PartitionSpec as P

D = 8192
STEPS = 3


EPS = 1e-06


def on_device(
    inputs,
    in_gain,
    qkv_weight,
    decay,
    state,
    head_gain,
    out_weight,
    mid_gain,
    up_weight,
    down_weight,
    att_mask,
    ffn_mask,
):
    batch_count = lax.axis_size("batch")
    tensor_count = lax.axis_size("tensor")
    total_rows = inputs.shape[1]
    my_rows = total_rows // batch_count
    share_rows = total_rows // tensor_count
    heads_here = decay.shape[0]
    head_size = state.shape[-1]
    scale = head_size ** (-0.5)
    row_start = lax.axis_index("tensor") * share_rows
    carried = state
    results = []
    for step in range(STEPS):
        current = inputs[step].astype(jnp.float32)
        squares = lax.psum(jnp.sum(current * current, axis=-1), "batch")
        normed = (current * in_gain * lax.rsqrt(squares / D + EPS)[:, None]).astype(jnp.bfloat16)
        projected = lax.psum_scatter(
            jnp.dot(normed, qkv_weight, preferred_element_type=jnp.float32),
            "batch",
            scatter_dimension=0,
            tiled=True,
        )
        projected = projected.reshape(my_rows, heads_here, 3, head_size)
        queries = projected[:, :, 0, :] * scale
        keys_now = projected[:, :, 1, :] * scale
        values_now = projected[:, :, 2, :]
        carried = decay[None, :, None, None] * carried + jnp.einsum(
            "rhi,rhj->rhij", keys_now, values_now, precision=lax.Precision.HIGHEST
        )
        attended = jnp.einsum("rhi,rhij->rhj", queries, carried, precision=lax.Precision.HIGHEST)
        attended = attended * lax.rsqrt(jnp.mean(attended * attended, axis=-1, keepdims=True) + EPS)
        spiked = (
            attended.reshape(my_rows, heads_here * head_size) * head_gain * att_mask[step]
        ).astype(jnp.bfloat16)
        partial_out = jnp.dot(
            lax.all_gather(spiked, "batch", axis=0, tiled=True),
            out_weight,
            preferred_element_type=jnp.float32,
        )
        mixed = current + lax.psum(partial_out, "tensor")
        mixed_squares = lax.psum(jnp.sum(mixed * mixed, axis=-1), "batch")
        hidden_in = (mixed * mid_gain * lax.rsqrt(mixed_squares / D + EPS)[:, None]).astype(
            jnp.bfloat16
        )
        kept = lax.dynamic_slice_in_dim(mixed, row_start, share_rows, 0)
        gate_sum = lax.psum_scatter(
            jnp.dot(hidden_in, up_weight, preferred_element_type=jnp.float32),
            "batch",
            scatter_dimension=0,
            tiled=True,
        )
        fired = (ffn_mask[step] * jax.nn.silu(gate_sum)).astype(jnp.bfloat16)
        ffn_part = jnp.dot(
            lax.all_gather(fired, "batch", axis=0, tiled=True),
            down_weight,
            preferred_element_type=jnp.float32,
        )
        final = kept + lax.psum_scatter(ffn_part, "tensor", scatter_dimension=0, tiled=True)
        results.append(final.astype(jnp.bfloat16))
    return jnp.stack(results)


def solution(mesh):
    return jax.shard_map(
        on_device,
        mesh=mesh,
        in_specs=(
            P(None, None, "batch"),
            P("batch"),
            P("batch", "tensor"),
            P("tensor"),
            P("batch", "tensor", None, None),
            P("tensor"),
            P("tensor", "batch"),
            P("batch"),
            P("batch", "tensor"),
            P("tensor", "batch"),
            P(None, "batch", "tensor"),
            P(None, "batch", "tensor"),
        ),
        out_specs=P(None, "tensor", "batch"),
        check_vma=False,
    )
```

profile of v0, /device:TPU:96, one launch (start us, length us, event | category | flops | bytes accessed | tf_op | source)
XLA Modules:
  0.0 855.4 jit_solution(16216907900491491913)
XLA Ops:
  8.0 22.7 %all-reduce.2 = (f32[256]{0:T(256)S(1)}, f32[256]{0:T(256)S(1)}, f32[256]{0:T(256)S(1)}) all-reduce(f32[256]{0:T(256)S(1)} %get-tuple-element.7, f32[256]{0:T(256)S(1)} %get-tuple-element.6, f32[256]{0:T(256)S(1)} %get-tuple-element.5), channel_id=1, replica_groups=mesh['batch'=16,'tensor'=16] {'batch'}, use_global_device_ids=true, to_apply=%region_19.20 | all-reduce | flops 768 | bytes 6144 | tf_op jit(solution)/shard_map/psum | solution.py:40
  30.8 3.3 fusion.37
  39.8 51.7 %reduce-scatter.10.cloned.1.call-done = f32[16,1536]{1,0:T(8,128)} async-done(((f32[256,1536]{1,0:T(8,128)}), f32[16,1536]{1,0:T(8,128)}) %reduce-scatter.10.cloned.1.call-update) | async-done | bytes 98320 | tf_op jit(solution)/shard_map/reduce_scatter | solution.py:42
  92.4 58.5 %reduce-scatter.16.cloned.1.call-done = f32[16,1536]{1,0:T(8,128)} async-done(((f32[256,1536]{1,0:T(8,128)}), f32[16,1536]{1,0:T(8,128)}) %reduce-scatter.16.cloned.1.call-update) | async-done | bytes 98320 | tf_op jit(solution)/shard_map/reduce_scatter | solution.py:42
  152.0 58.1 %reduce-scatter.22.cloned.1.call-done = f32[16,1536]{1,0:T(8,128)} async-done(((f32[256,1536]{1,0:T(8,128)}), f32[16,1536]{1,0:T(8,128)}) %reduce-scatter.22.cloned.1.call-update) | async-done | bytes 98320 | tf_op jit(solution)/shard_map/reduce_scatter | solution.py:42
  211.2 5.9 fusion.4
  217.1 5.7 fusion.5
  222.8 6.8 fusion
  230.3 17.2 %all_gather.18 = bf16[256,512]{1,0:T(8,128)(2,1)S(1)} all-gather(bf16[16,512]{1,0:T(8,128)(2,1)S(1)} %get-tuple-element.36), channel_id=1, replica_groups=mesh['batch'=16,'tensor'=16] {'batch'}, dimensions={0}, use_global_device_ids=true | all-gather | bytes 278528 | tf_op jit(solution)/shard_map/all_gather | solution.py:61
  247.5 14.9 %all_gather.20 = bf16[256,512]{1,0:T(8,128)(2,1)S(1)} all-gather(bf16[16,512]{1,0:T(8,128)(2,1)S(1)} %get-tuple-element.38), channel_id=1, replica_groups=mesh['batch'=16,'tensor'=16] {'batch'}, dimensions={0}, use_global_device_ids=true | all-gather | bytes 278528 | tf_op jit(solution)/shard_map/all_gather | solution.py:61
  264.6 16.8 %all_gather.22 = bf16[256,512]{1,0:T(8,128)(2,1)S(1)} all-gather(bf16[16,512]{1,0:T(8,128)(2,1)S(1)} %get-tuple-element.37), channel_id=1, replica_groups=mesh['batch'=16,'tensor'=16] {'batch'}, dimensions={0}, use_global_device_ids=true | all-gather | bytes 278528 | tf_op jit(solution)/shard_map/all_gather | solution.py:61
  282.6 99.6 %all-reduce.5.cloned.1.call-done = (f32[256,512]{1,0:T(8,128)}, f32[256,512]{1,0:T(8,128)}, f32[256,512]{1,0:T(8,128)}) async-done(((f32[256,512]{1,0:T(8,128)}, f32[256,512]{1,0:T(8,128)}, f32[256,512]{1,0:T(8,128)}), (f32[256,512]{1,0:T(8,128)}, f32[256,512]{1,0:T(8,128)}, f32[256,512]{1,0:T(8,128)})) %all-reduce.5.cloned.1.call-update) | async-done | bytes 1572880 | tf_op jit(solution)/shard_map/psum | solution.py:65
  384.7 22.4 %all-reduce.1 = (f32[256]{0:T(256)S(1)}, f32[256]{0:T(256)S(1)}, f32[256]{0:T(256)S(1)}) all-reduce(f32[256]{0:T(256)S(1)} %get-tuple-element.25, f32[256]{0:T(256)S(1)} %get-tuple-element.23, f32[256]{0:T(256)S(1)} %get-tuple-element.17), channel_id=1, replica_groups=mesh['batch'=16,'tensor'=16] {'batch'}, use_global_device_ids=true, to_apply=%region_24.25 | all-reduce | flops 768 | bytes 6144 | tf_op jit(solution)/shard_map/psum | solution.py:66
  407.1 3.0 fusion.31
  414.2 51.7 %reduce-scatter.18.cloned.1.call-done = f32[16,1792]{1,0:T(8,128)} async-done(((f32[256,1792]{1,0:T(8,128)}), f32[16,1792]{1,0:T(8,128)}) %reduce-scatter.18.cloned.1.call-update) | async-done | bytes 114704 | tf_op jit(solution)/shard_map/reduce_scatter | solution.py:71
  465.9 59.8 %reduce-scatter.24.cloned.1.call-done = f32[16,1792]{1,0:T(8,128)} async-done(((f32[256,1792]{1,0:T(8,128)}), f32[16,1792]{1,0:T(8,128)}) %reduce-scatter.24.cloned.1.call-update) | async-done | bytes 114704 | tf_op jit(solution)/shard_map/reduce_scatter | solution.py:71
  525.7 59.7 %reduce-scatter.12.cloned.1.call-done = f32[16,1792]{1,0:T(8,128)} async-done(((f32[256,1792]{1,0:T(8,128)}), f32[16,1792]{1,0:T(8,128)}) %reduce-scatter.12.cloned.1.call-update) | async-done | bytes 114704 | tf_op jit(solution)/shard_map/reduce_scatter | solution.py:71
  586.4 19.0 %all_gather.19 = bf16[256,1792]{1,0:T(8,128)(2,1)S(1)} all-gather(bf16[16,1792]{1,0:T(8,128)(2,1)S(1)} %get-tuple-element.27), channel_id=1, replica_groups=mesh['batch'=16,'tensor'=16] {'batch'}, dimensions={0}, use_global_device_ids=true | all-gather | bytes 974848 | tf_op jit(solution)/shard_map/all_gather | solution.py:79
  608.5 17.0 %all_gather.21 = bf16[256,1792]{1,0:T(8,128)(2,1)S(1)} all-gather(bf16[16,1792]{1,0:T(8,128)(2,1)S(1)} %get-tuple-element.29), channel_id=1, replica_groups=mesh['batch'=16,'tensor'=16] {'batch'}, dimensions={0}, use_global_device_ids=true | all-gather | bytes 974848 | tf_op jit(solution)/shard_map/all_gather | solution.py:79
  625.6 3.0 fusion.84
  628.6 18.3 %all_gather.23 = bf16[256,1792]{1,0:T(8,128)(2,1)S(1)} all-gather(bf16[16,1792]{1,0:T(8,128)(2,1)S(1)} %get-tuple-element.28), channel_id=1, replica_groups=mesh['batch'=16,'tensor'=16] {'batch'}, dimensions={0}, use_global_device_ids=true | all-gather | bytes 974848 | tf_op jit(solution)/shard_map/all_gather | solution.py:79
  649.8 36.5 %reduce-scatter.14.cloned.1.call-done = f32[16,512]{1,0:T(8,128)} async-done(((f32[256,512]{1,0:T(8,128)}), f32[16,512]{1,0:T(8,128)}) %reduce-scatter.14.cloned.1.call-update) | async-done | bytes 32784 | tf_op jit(solution)/shard_map/reduce_scatter | solution.py:83
  687.1 79.9 %reduce-scatter.20.cloned.1.call-done = f32[16,512]{1,0:T(8,128)} async-done(((f32[256,512]{1,0:T(8,128)}), f32[16,512]{1,0:T(8,128)}) %reduce-scatter.20.cloned.1.call-update) | async-done | bytes 32784 | tf_op jit(solution)/shard_map/reduce_scatter | solution.py:83
  767.8 79.4 %reduce-scatter.26.cloned.1.call-done = f32[16,512]{1,0:T(8,128)} async-done(((f32[256,512]{1,0:T(8,128)}), f32[16,512]{1,0:T(8,128)}) %reduce-scatter.26.cloned.1.call-update) | async-done | bytes 32784 | tf_op jit(solution)/shard_map/reduce_scatter | solution.py:83
  (82 shorter events, 30.9 us)
Async XLA Ops:
  6.5 400.5 %copy-start = (bf16[512,1792]{1,0:T(8,128)(2,1)S(1)}, bf16[512,1792]{1,0:T(8,128)(2,1)}, u32[]{:S(2)}) copy-start(bf16[512,1792]{1,0:T(8,128)(2,1)} %param.20) | copy-start | bytes 5505028
  6.5 27.6 %copy-start.9 = (f32[512]{0:T(512)S(1)}, f32[512]{0:T(512)}, u32[]{:S(2)}) copy-start(f32[512]{0:T(512)} %param.13) | copy-start | bytes 6148
  6.5 27.6 %copy-start.1 = (bf16[512,1536]{1,0:T(8,128)(2,1)S(1)}, bf16[512,1536]{1,0:T(8,128)(2,1)}, u32[]{:S(2)}) copy-start(bf16[512,1536]{1,0:T(8,128)(2,1)} %param.14) | copy-start | bytes 4718596
  6.5 84.9 %reduce-scatter.10.cloned.1.call-start = ((), (), s32[]{:S(2)}) async-start(), calls=%async_computation.9 | async-start | bytes 1671168 | tf_op jit(solution)/shard_map/reduce_scatter | solution.py:42
  34.1 116.8 %reduce-scatter.16.cloned.1.call-start = ((), (), s32[]{:S(2)}) async-start(), calls=%async_computation.12 | async-start | bytes 1671168 | tf_op jit(solution)/shard_map/reduce_scatter | solution.py:42
  36.9 174.3 %copy-start.11 = (f32[4]{0:T(128)S(1)}, f32[4]{0:T(128)}, u32[]{:S(2)}) copy-start(f32[4]{0:T(128)} %param.15) | copy-start | bytes 52
  36.9 173.2 %reduce-scatter.22.cloned.1.call-start = ((), (), s32[]{:S(2)}) async-start(), calls=%async_computation.15 | async-start | bytes 1671168 | tf_op jit(solution)/shard_map/reduce_scatter | solution.py:42
  39.7 342.5 %all-reduce.5.cloned.1.call-start = ((), (), s32[]{:S(2)}) async-start(), calls=%async_computation.18 | async-start | bytes 3145728 | tf_op jit(solution)/shard_map/psum | solution.py:65
  211.1 6.0 copy-start.4
  222.8 7.4 copy-start.7
  222.8 7.4 copy-start.10
  222.8 39.5 %copy-start.3 = (bf16[512,512]{1,0:T(8,128)(2,1)S(1)}, bf16[512,512]{1,0:T(8,128)(2,1)}, u32[]{:S(2)}) copy-start(bf16[512,512]{1,0:T(8,128)(2,1)} %param.18) | copy-start | bytes 1572868
  229.6 152.6 %copy-start.2 = (bf16[3,256,512]{2,1,0:T(8,128)(2,1)S(1)}, bf16[3,256,512]{2,1,0:T(8,128)(2,1)}, u32[]{:S(2)}) copy-start(bf16[3,256,512]{2,1,0:T(8,128)(2,1)} %param.12) | copy-start | bytes 2359300
  263.5 143.6 %copy-start.8 = (f32[512]{0:T(512)S(1)}, f32[512]{0:T(512)}, u32[]{:S(2)}) copy-start(f32[512]{0:T(512)} %param.19) | copy-start | bytes 6148
  282.5 183.4 %reduce-scatter.18.cloned.1.call-start = ((), (), s32[]{:S(2)}) async-start(), calls=%async_computation.13 | async-start | bytes 1949696 | tf_op jit(solution)/shard_map/reduce_scatter | solution.py:71
  410.0 2.1 copy-start.5
  410.1 115.6 %reduce-scatter.24.cloned.1.call-start = ((), (), s32[]{:S(2)}) async-start(), calls=%async_computation.16 | async-start | bytes 1949696 | tf_op jit(solution)/shard_map/reduce_scatter | solution.py:71
  412.1 173.3 %copy-start.6 = (s32[3,16,1792]{2,1,0:T(8,128)S(1)}, s32[3,16,1792]{2,1,0:T(8,128)}, u32[]{:S(2)}) copy-start(s32[3,16,1792]{2,1,0:T(8,128)} %param.23) | copy-start | bytes 1032196
  412.1 173.2 %reduce-scatter.12.cloned.1.call-start = ((), (), s32[]{:S(2)}) async-start(), calls=%async_computation.10 | async-start | bytes 1949696 | tf_op jit(solution)/shard_map/reduce_scatter | solution.py:71
  414.1 272.2 %reduce-scatter.14.cloned.1.call-start = ((), (), s32[]{:S(2)}) async-start(), calls=%async_computation.11 | async-start | bytes 557056 | tf_op jit(solution)/shard_map/reduce_scatter | solution.py:83
  608.5 158.5 %reduce-scatter.20.cloned.1.call-start = ((), (), s32[]{:S(2)}) async-start(), calls=%async_computation.14 | async-start | bytes 557056 | tf_op jit(solution)/shard_map/reduce_scatter | solution.py:83
  628.5 218.6 %reduce-scatter.26.cloned.1.call-start = ((), (), s32[]{:S(2)}) async-start(), calls=%async_computation.17 | async-start | bytes 557056 | tf_op jit(solution)/shard_map/reduce_scatter | solution.py:83
Sparse Core Ops, SparseCore 0:
  34.2 57.2 reduce-scatter.9
  94.2 56.6 reduce-scatter.15
  153.4 56.6 reduce-scatter.21
  282.6 99.5 all-reduce.4
  410.2 55.6 reduce-scatter.17
  468.3 57.3 reduce-scatter.23
  528.4 56.9 reduce-scatter.11
  608.6 77.6 reduce-scatter.13
  690.2 76.7 reduce-scatter.19
  770.3 76.7 reduce-scatter.25
where the time goes:
time: 857 us; the launch traced here: 855 us
  waiting for transfers between devices  635 us (74%)
  blocking collectives  148 us (17%)
  matrix products  46.1 us (5%)
  between operations  13.8 us (2%)
  other arithmetic  8.84 us (1%)
    reduce_scatter x3, waiting for transfers between devices, on_device(): lax.psum_scatter(ffn_part, 'tensor', scatter_dimension=0, tiled=True)  196 us
    reduce_scatter x3, waiting for transfers between devices, on_device(): lax.psum_scatter(jnp.dot(hidden_in, up_weight, preferred_element_type=jnp...  171 us
    reduce_scatter x3, waiting for transfers between devices, on_device(): lax.psum_scatter(jnp.dot(normed, qkv_weight, preferred_element_type=jnp.f...  168 us
    psum x1, waiting for transfers between devices, on_device(): mixed = current + lax.psum(partial_out, 'tensor')  99.6 us
    all_gather x3, blocking collectives, on_device(): lax.all_gather(fired, 'batch', axis=0, tiled=True)  54.3 us
    all_gather x3, blocking collectives, on_device(): lax.all_gather(spiked, 'batch', axis=0, tiled=True)  48.9 us
    psum x1, blocking collectives, on_device(): squares = lax.psum(jnp.sum(current * current, axis=-1), 'batch')  22.7 us
    psum x1, blocking collectives, on_device(): mixed_squares = lax.psum(jnp.sum(mixed * mixed, axis=-1), 'batch')  22.4 us
  transfers between devices with their start and end apart: 10, of which 10 were waited for; matrix products, arithmetic and copies ran while one was open for 2% of the time, Pallas kernels for 0%

commit v1 on v0

v1 whole, which is shorter than its diff:
```python
import functools

import jax
import jax.numpy as jnp
from jax import lax
from jax.experimental import pallas as pl
from jax.experimental.pallas import tpu as pltpu
from jax.sharding import Mesh
from jax.sharding import PartitionSpec as P

D = 8192
STEPS = 3
DH = 128
EPS = 1e-06
LANES = 128
BATCH = ("z", "core")
TENSOR = ("y", "xh", "xl")
TENSOR_ROWS = ("xl", "y", "xh")


def pieces_of(sums):
    high = lax.reduce_precision(sums, 8, 7)
    middle = lax.reduce_precision(sums - high, 8, 7)
    low = sums - high - middle
    lane = lax.broadcasted_iota(jnp.int32, sums.shape[:-1] + (LANES,), sums.ndim - 1)
    out = jnp.where(lane == 0, high, jnp.where(lane == 1, middle, jnp.where(lane == 2, low, 0.0)))
    return out.astype(jnp.bfloat16)


def swap_cores(value):
    return lax.ppermute(value, "core", [(0, 1), (1, 0)])


def attention_kernel(decay_ref, parts_ref, sums_ref, state_ref, gain_ref, mask_ref, out_ref):
    head = pl.program_id(0)
    rows = parts_ref.shape[1]
    mine = rows // STEPS
    squares = jnp.sum(jnp.sum(sums_ref[...].astype(jnp.float32), axis=0), axis=-1, keepdims=True)
    inverse = lax.rsqrt(squares / D + EPS)
    parts = jnp.sum(parts_ref[...].astype(jnp.float32), axis=0) * inverse
    scale = DH ** (-0.5)
    queries = parts[:, :DH] * scale
    keys = parts[:, DH : 2 * DH] * scale
    values = parts[:, 2 * DH :]
    rate = decay_ref[head]
    turned = queries.T
    found = [[] for _ in range(STEPS)]
    for request in range(mine):
        block = state_ref[request, 0]
        for step in range(STEPS):
            at = step * mine + request
            found[step].append(jnp.sum(turned[:, at : at + 1] * block, axis=0, keepdims=True))
    power = rate
    for step in range(STEPS):
        here = slice(step * mine, (step + 1) * mine)
        total = power * jnp.concatenate(found[step], axis=0)
        power = power * rate
        factor = None
        for earlier in range(step, -1, -1):
            there = slice(earlier * mine, (earlier + 1) * mine)
            score = jnp.sum(queries[here] * keys[there], axis=-1, keepdims=True)
            if factor is not None:
                score = score * factor
            total = total + score * values[there]
            factor = rate if factor is None else factor * rate
        total = total * lax.rsqrt(jnp.mean(total * total, axis=-1, keepdims=True) + EPS)
        spiked = total * gain_ref[...] * mask_ref[step].astype(jnp.float32)
        out_ref[here, :] = spiked.astype(jnp.bfloat16)


def attention(decay, parts, state, head_gain, att_mask):
    sources, rows, width = parts.shape
    mine, heads = state.shape[:2]
    last = width // LANES - 1
    return pl.pallas_call(
        attention_kernel,
        grid=(heads,),
        in_specs=[
            pl.BlockSpec(memory_space=pltpu.SMEM),
            pl.BlockSpec((sources, rows, 3 * DH), lambda h: (0, 0, h)),
            pl.BlockSpec((sources, rows, LANES), lambda h: (0, 0, last)),
            pl.BlockSpec((mine, 1, DH, DH), lambda h: (0, h, 0, 0)),
            pl.BlockSpec((1, DH), lambda h: (0, h)),
            pl.BlockSpec((STEPS, mine, DH), lambda h: (0, 0, h)),
        ],
        out_specs=pl.BlockSpec((rows, DH), lambda h: (0, h)),
        out_shape=jax.ShapeDtypeStruct((rows, heads * DH), jnp.bfloat16),
        compiler_params=pltpu.CompilerParams(vmem_limit_bytes=32 * 1024 * 1024),
    )(decay, parts, parts, state, head_gain[None, :], att_mask)


def sum_to_owner(rows, weight, sums, core):
    cores, zs, each, depth = rows.shape
    width = weight.shape[1]

    def product(which):
        picked = lax.dynamic_index_in_dim(rows, which, 0, keepdims=False).reshape(zs * each, depth)
        return jnp.dot(picked, weight, preferred_element_type=jnp.float32).astype(jnp.bfloat16)

    theirs = swap_cores(product(1 - core))
    their_sums = swap_cores(lax.dynamic_index_in_dim(sums, 1 - core, 0, keepdims=False))
    ours = product(core)
    total = (ours.astype(jnp.float32) + theirs.astype(jnp.float32)).astype(jnp.bfloat16)
    squares = lax.dynamic_index_in_dim(sums, core, 0, keepdims=False) + their_sums
    sent = jnp.concatenate([total.reshape(zs, each, width), pieces_of(squares)], axis=-1)
    return lax.all_to_all(sent, "z", 0, 0, tiled=True)


def gather_rows(value, zs):
    along_z = lax.all_to_all(jnp.broadcast_to(value[None], (zs,) + value.shape), "z", 0, 0, tiled=True)
    both = lax.all_gather(along_z, "core", axis=0, tiled=False)
    return both.reshape(2 * zs * value.shape[0], value.shape[1])


def on_device(
    inputs,
    in_gain,
    qkv_weight,
    decay,
    state,
    head_gain,
    out_weight,
    mid_gain,
    up_weight,
    down_weight,
    att_mask,
    ffn_mask,
):
    cores = lax.axis_size("core")
    zs = lax.axis_size("z")
    core = lax.axis_index("core")
    share = inputs.shape[1] // (zs * cores)
    features = inputs.shape[2]
    each = STEPS * share
    ordered = inputs.reshape(STEPS, zs, cores, share, features).transpose(2, 1, 0, 3, 4)
    current = ordered.reshape(cores, zs, each, features).astype(jnp.float32)
    squares = jnp.sum(current * current, axis=-1, keepdims=True)
    scaled = (current * in_gain).astype(jnp.bfloat16)
    parts = sum_to_owner(scaled, qkv_weight, squares, core)
    spiked = attention(decay, parts, state, head_gain, att_mask)

    everyone = gather_rows(spiked, zs)
    partial = jnp.dot(everyone, out_weight, preferred_element_type=jnp.float32).astype(jnp.bfloat16)
    partial = lax.all_to_all(partial.reshape(cores * zs, each, features), TENSOR_ROWS, 0, 0, tiled=True)
    start = lax.axis_index(TENSOR) * share
    kept = lax.dynamic_slice_in_dim(inputs, start, share, 1).reshape(each, features).astype(jnp.float32)
    mixed = kept + jnp.sum(partial.astype(jnp.float32), axis=0)

    hidden = (mixed * mid_gain).astype(jnp.bfloat16)
    hidden = jnp.broadcast_to(hidden[None], (cores * zs, each, features))
    hidden = lax.all_to_all(hidden, TENSOR_ROWS, 0, 0, tiled=True)
    hidden = hidden.reshape(cores, zs, each, features)
    back = hidden.astype(jnp.float32) * (1.0 / mid_gain)
    squares = jnp.sum(back * back, axis=-1, keepdims=True)
    parts = sum_to_owner(hidden, up_weight, squares, core)
    total = jnp.sum(parts.astype(jnp.float32), axis=0)
    units = up_weight.shape[1]
    inverse = lax.rsqrt(jnp.sum(total[:, units:], axis=-1, keepdims=True) / D + EPS)
    gate = total[:, :units] * inverse
    fired = ffn_mask.reshape(each, units) * (gate / (1.0 + jnp.exp(-gate)))

    everyone = gather_rows(fired.astype(jnp.bfloat16), zs)
    partial = jnp.dot(everyone, down_weight, preferred_element_type=jnp.float32).astype(jnp.bfloat16)
    partial = lax.all_to_all(partial.reshape(cores * zs, each, features), TENSOR_ROWS, 0, 0, tiled=True)
    final = mixed + jnp.sum(partial.astype(jnp.float32), axis=0)
    return final.astype(jnp.bfloat16).reshape(STEPS, share, features)


def solution(mesh):
    devices = mesh.devices.reshape(8, 2, 4, 2, 2)
    inner = Mesh(devices, ("z", "core", "y", "xh", "xl"))
    return jax.shard_map(
        on_device,
        mesh=inner,
        in_specs=(
            P(None, None, BATCH),
            P(BATCH),
            P(BATCH, TENSOR),
            P(TENSOR),
            P(BATCH, TENSOR, None, None),
            P(TENSOR),
            P(TENSOR, BATCH),
            P(BATCH),
            P(BATCH, TENSOR),
            P(TENSOR, BATCH),
            P(None, BATCH, TENSOR),
            P(None, BATCH, TENSOR),
        ),
        out_specs=P(None, TENSOR, BATCH),
        check_vma=False,
    )
```

time: 857 us -> 256 us (0.30)
  waiting for transfers between devices: 635 us -> 30.2 us
  matrix products: 46.1 us -> 11.4 us
  blocking collectives: 148 us -> 176 us
    reduce_scatter x9 -> x0, waiting for transfers between devices: 535 us -> none  [the longest x3 196 us: on_device(): lax.psum_scatter(ffn_part, 'tensor', scatter_dimension=0, tiled=True)]
    all_to_all x0 -> x6, blocking collectives: none -> 174 us  [the longest x2 78.9 us: sum_to_owner(): return lax.all_to_all(sent, 'z', 0, 0, tiled=True)]
    all_gather x6 -> x1, blocking collectives: 103 us -> 2.36 us  [gather_rows(): both = lax.all_gather(along_z, 'core', axis=0, tiled=False)]
    psum x1 -> x0, waiting for transfers between devices: 99.6 us -> none  [on_device(): mixed = current + lax.psum(partial_out, 'tensor')]
    psum x2 -> x0, blocking collectives: 45.1 us -> none  [the longest x1 22.7 us: on_device(): squares = lax.psum(jnp.sum(current * current, axis=-1), 'batch')]
    dot_general x15 -> x6, matrix products: 46.1 us -> 11.4 us  [the longest x4 6.09 us: product(): jnp.dot(picked, weight, preferred_element_type=jnp.float32)]
    all_to_all x0 -> x1, waiting for transfers between devices: none -> 13.1 us  [on_device(): lax.all_to_all(partial.reshape(cores * zs, each, features), TENSOR_ROWS,...]
    all_gather x0 -> x1, waiting for transfers between devices: none -> 12.9 us  [gather_rows(): both = lax.all_gather(along_z, 'core', axis=0, tiled=False)]
  transfers between devices with their start and end apart: 10 -> 6, of which waited for: 10 -> 5; matrix products, arithmetic and copies ran while one was open for 2% -> 1% of each run, Pallas kernels for 0% -> 0%
where the time goes in v1:
time: 256 us; the launch traced here: 255 us
  blocking collectives  176 us (69%)
  waiting for transfers between devices  30.2 us (12%)
  between operations  13.7 us (5%)
  matrix products  11.4 us (4%)
  starting transfers between devices  8.43 us (3%)
  Pallas kernels  6.57 us (3%)
  other arithmetic  5.8 us (2%)
  local copies, waits for them, and re-layouts  3.02 us (1%)
    all_to_all x2, blocking collectives, sum_to_owner(): return lax.all_to_all(sent, 'z', 0, 0, tiled=True)  78.9 us
    all_to_all x2, blocking collectives, gather_rows(): lax.all_to_all(jnp.broadcast_to(value[None], (zs,) + value.shape), 'z', 0...  55.9 us
    all_to_all x1, blocking collectives, on_device(): lax.all_to_all(partial.reshape(cores * zs, each, features), TENSOR_ROWS,...  21.3 us
    all_to_all x1, blocking collectives, on_device(): hidden = lax.all_to_all(hidden, TENSOR_ROWS, 0, 0, tiled=True)  17.5 us
    all_to_all x1, waiting for transfers between devices, on_device(): lax.all_to_all(partial.reshape(cores * zs, each, features), TENSOR_ROWS,...  13.1 us
    all_gather x1, waiting for transfers between devices, gather_rows(): both = lax.all_gather(along_z, 'core', axis=0, tiled=False)  12.9 us
    all_to_all x1, starting transfers between devices, on_device(): lax.all_to_all(partial.reshape(cores * zs, each, features), TENSOR_ROWS,...  7.17 us
    pallas_call x1, Pallas kernels, attention(): pl.pallas_call(attention_kernel, grid=(heads,), in_specs=[pl.BlockSpec(me...  6.57 us
  transfers between devices with their start and end apart: 6, of which 5 were waited for; matrix products, arithmetic and copies ran while one was open for 1% of the time, Pallas kernels for 0%

profile of v1, /device:TPU:96, one launch (start us, length us, event | category | flops | bytes accessed | tf_op | source)
XLA Modules:
  0.0 255.1 jit_solution(18309580531714266373)
XLA Ops:
  6.5 1.5 convert_element_type.143
  9.0 1.1 copy-done.9
  10.1 1.8 convolution_convert_fusion
  12.9 1.8 collective-permute-done.1
  15.1 2.5 add_convert_fusion.1
  17.8 38.1 %all_to_all.35.parts_ref.sums_ref = bf16[8,48,1664]{2,1,0:T(8,128)(2,1)S(1)} all-to-all(bf16[8,48,1664]{2,1,0:T(8,128)(2,1)S(1)} %pad_maximum_fusion.1), channel_id=1, replica_groups=mesh['z'=8,'core'=2,'y'=4,'xh'=2,'xl'=2] {'z'}, dimensions={0} | all-to-all | bytes 2555904 | tf_op jit(solution)/shard_map/all_to_all | solution.py:106
  55.9 6.6 %shard_map.118 = bf16[48,512]{1,0:T(8,128)(2,1)S(1)} custom-call(f32[4]{0:T(128)S(1)} %copy-done.4, bf16[8,48,1664]{2,1,0:T(8,128)(2,1)S(1)} %all_to_all.35.parts_ref.sums_ref, bf16[8,48,1664]{2,1,0:T(8,128)(2,1)S(1)} %all_to_all.35.parts_ref.sums_ref, f32[16,4,128,128]{3,2,1,0:T(8,128)S(1)} %copy-done.1, f32[1,512]{1,0:T(1,128)S(1)} %bitcast.67, ...), custom_call_target="tpu_custom_call" | custom-call | tf_op jit(solution)/shard_map/pallas_call | solution.py:75
  62.6 16.5 %all_to_all.36 = bf16[8,48,512]{2,1,0:T(8,128)(2,1)S(1)} all-to-all(bf16[8,48,512]{2,1,0:T(8,128)(2,1)S(1)} %broadcast_in_dim.88), channel_id=1, replica_groups=mesh['z'=8,'core'=2,'y'=4,'xh'=2,'xl'=2] {'z'}, dimensions={0} | all-to-all | bytes 786432 | tf_op jit(solution)/shard_map/all_to_all | solution.py:110
  79.0 2.4 all-gather
  81.4 1.4 convolution_convert_fusion.5
  82.8 7.2 %all-to-all-start.2 = ((bf16[16,48,512]{2,1,0:T(8,128)(2,1)}), bf16[16,48,512]{2,1,0:T(8,128)(2,1)S(1)}, u32[]{:S(2)}, u32[]{:S(2)}) async-start(bf16[16,48,512]{2,1,0:T(8,128)(2,1)} %bitcast.73), calls=%async_computation.2 | async-start | bytes 1572864 | tf_op jit(solution)/shard_map/all_to_all | solution.py:144
  90.1 0.7 dynamic-slice_convert_fusion
  90.7 13.1 %all-to-all-done.2 = bf16[16,48,512]{2,1,0:T(8,128)(2,1)S(1)} async-done(((bf16[16,48,512]{2,1,0:T(8,128)(2,1)}), bf16[16,48,512]{2,1,0:T(8,128)(2,1)S(1)}, u32[]{:S(2)}, u32[]{:S(2)}) %all-to-all-start.2) | async-done | bytes 786464 | tf_op jit(solution)/shard_map/all_to_all | solution.py:144
  104.0 0.9 fusion.5
  105.0 17.5 %all_to_all.37 = bf16[16,48,512]{2,1,0:T(8,128)(2,1)S(1)} all-to-all(bf16[16,48,512]{2,1,0:T(8,128)(2,1)S(1)} %broadcast_in_dim.89), channel_id=1, replica_groups=mesh['z'=8,'core'=2,'y'=4,'xh'=2,'xl'=2] {'xl','y','xh'}, dimensions={0} | all-to-all | bytes 1572864 | tf_op jit(solution)/shard_map/all_to_all | solution.py:151
  122.6 0.9 convolution_convert_fusion.2
  124.4 2.2 collective-permute-done.3
  126.9 0.9 add_convert_fusion
  127.9 40.8 %all_to_all.38 = bf16[8,48,1920]{2,1,0:T(8,128)(2,1)S(1)} all-to-all(bf16[8,48,1920]{2,1,0:T(8,128)(2,1)S(1)} %pad_maximum_fusion), channel_id=1, replica_groups=mesh['z'=8,'core'=2,'y'=4,'xh'=2,'xl'=2] {'z'}, dimensions={0} | all-to-all | bytes 2949120 | tf_op jit(solution)/shard_map/all_to_all | solution.py:106
  169.1 0.7 copy-done.6
  170.0 39.4 %all_to_all.39 = bf16[8,48,1792]{2,1,0:T(8,128)(2,1)} all-to-all(bf16[8,48,1792]{2,1,0:T(8,128)(2,1)S(1)} %broadcast_in_dim.96), channel_id=1, replica_groups=mesh['z'=8,'core'=2,'y'=4,'xh'=2,'xl'=2] {'z'}, dimensions={0} | all-to-all | bytes 2752512 | tf_op jit(solution)/shard_map/all_to_all | solution.py:110
  209.4 12.9 %all-gather.4.cloned.1.call-done = bf16[16,48,1792]{2,1,0:T(8,128)(2,1)} async-done(((bf16[8,48,1792]{2,1,0:T(8,128)(2,1)}), bf16[16,48,1792]{2,1,0:T(8,128)(2,1)}) %all-gather.4.cloned.1.call-update) | async-done | bytes 2752528 | tf_op jit(solution)/shard_map/all_gather | solution.py:111
  222.3 3.9 %convolution_convert_fusion.4 = bf16[768,512]{1,0:T(8,128)(2,1)S(1)} fusion(bf16[768,1792]{1,0:T(8,128)(2,1)} %bitcast.84, bf16[1792,512]{1,0:T(8,128)(2,1)} %param.21), kind=kOutput, calls=%fused_computation.16 | convolution fusion | flops 1409679360 | bytes 5373952 | tf_op jit(solution)/shard_map/dot_general | solution.py:163
  226.2 21.3 %all_to_all.40 = bf16[16,48,512]{2,1,0:T(8,128)(2,1)S(1)} all-to-all(bf16[16,48,512]{2,1,0:T(8,128)(2,1)S(1)} %bitcast.75), channel_id=1, replica_groups=mesh['z'=8,'core'=2,'y'=4,'xh'=2,'xl'=2] {'xl','y','xh'}, dimensions={0} | all-to-all | bytes 1572864 | tf_op jit(solution)/shard_map/all_to_all | solution.py:164
  (60 shorter events, 5.4 us)
Async XLA Ops:
  6.5 116.0 %copy-start = (bf16[512,1792]{1,0:T(8,128)(2,1)S(1)}, bf16[512,1792]{1,0:T(8,128)(2,1)}, u32[]{:S(2)}) copy-start(bf16[512,1792]{1,0:T(8,128)(2,1)} %param.20) | copy-start | bytes 5505028
  8.0 0.7 copy-start.8
  8.7 1.4 copy-start.9
  10.1 1.8 copy-start.5
  11.9 3.2 %collective-permute-start = (bf16[384,1536]{1,0:T(8,128)(2,1)}, bf16[384,1536]{1,0:T(8,128)(2,1)}, u32[]{:S(2)}, u32[]{:S(2)}) collective-permute-start(bf16[384,1536]{1,0:T(8,128)(2,1)} %convolution_convert_fusion), channel_id=1, source_target_pairs={{0,16},{16,0},{1,17},{17,1},{2,18},{18,2},{3,19},{19,3},{4,20},{20... | collective-permute-start | bytes 3538952 | tf_op jit(solution)/shard_map/ppermute | solution.py:31
  12.4 2.4 collective-permute-start.1
  17.6 38.3 %copy-start.1 = (f32[16,4,128,128]{3,2,1,0:T(8,128)S(1)}, f32[16,4,128,128]{3,2,1,0:T(8,128)}, u32[]{:S(2)}) copy-start(f32[16,4,128,128]{3,2,1,0:T(8,128)} %state_ref.1) | copy-start | bytes 12582916
  17.8 38.2 %copy-start.2 = (s32[3,16,512]{2,1,0:T(8,128)S(1)}, s32[3,16,512]{2,1,0:T(8,128)}, u32[]{:S(2)}) copy-start(s32[3,16,512]{2,1,0:T(8,128)} %mask_ref.1) | copy-start | bytes 294916
  17.8 38.1 %copy-start.3 = (f32[512]{0:T(512)S(1)}, f32[512]{0:T(512)}, u32[]{:S(2)}) copy-start(f32[512]{0:T(512)} %param.17) | copy-start | bytes 6148
  17.8 38.1 %copy-start.4 = (f32[4]{0:T(128)S(1)}, f32[4]{0:T(128)}, u32[]{:S(2)}) copy-start(f32[4]{0:T(128)} %decay_ref.1) | copy-start | bytes 52
  62.5 18.9 %copy-start.10 = (bf16[512,512]{1,0:T(8,128)(2,1)S(1)}, bf16[512,512]{1,0:T(8,128)(2,1)}, u32[]{:S(2)}) copy-start(bf16[512,512]{1,0:T(8,128)(2,1)} %param.18) | copy-start | bytes 1572868
  82.8 21.1 %copy-start.7 = (f32[512]{0:T(512)S(1)}, f32[512]{0:T(512)}, u32[]{:S(2)}) copy-start(f32[512]{0:T(512)} %param.19) | copy-start | bytes 6148
  82.8 21.0 %all-to-all-start.2 = ((bf16[16,48,512]{2,1,0:T(8,128)(2,1)}), bf16[16,48,512]{2,1,0:T(8,128)(2,1)S(1)}, u32[]{:S(2)}, u32[]{:S(2)}) async-start(bf16[16,48,512]{2,1,0:T(8,128)(2,1)} %bitcast.73), calls=%async_computation.2 | async-start | bytes 1572864 | tf_op jit(solution)/shard_map/all_to_all | solution.py:144
  90.0 132.3 %all-gather.4.cloned.1.call-start = ((), (), s32[]{:S(2)}) async-start(), calls=%async_computation.7 | async-start | bytes 4128768 | tf_op jit(solution)/shard_map/all_gather | solution.py:111
  123.5 3.5 %collective-permute-start.2 = (bf16[384,1792]{1,0:T(8,128)(2,1)S(1)}, bf16[384,1792]{1,0:T(8,128)(2,1)S(1)}, u32[]{:S(2)}, u32[]{:S(2)}) collective-permute-start(bf16[384,1792]{1,0:T(8,128)(2,1)S(1)} %convolution_convert_fusion.2), channel_id=1, source_target_pairs={{0,16},{16,0},{1,17},{17,1},{2,18},{18,2},{3,19},{19,3},{4,20},{20... | collective-permute-start | bytes 4128776 | tf_op jit(solution)/shard_map/ppermute | solution.py:31
  123.9 2.8 %collective-permute-start.3 = (f32[8,48,1]{1,0,2:T(8,128)S(1)}, f32[8,48,1]{1,0,2:T(8,128)S(1)}, u32[]{:S(2)}, u32[]{:S(2)}) collective-permute-start(f32[8,48,1]{1,0,2:T(8,128)S(1)} %dynamic-slice_bitcast_fusion), channel_id=1, source_target_pairs={{0,16},{16,0},{1,17},{17,1},{2,18},{18,2},{3,19},{19,3},{4,20},{20... | collective-permute-start | bytes 4616 | tf_op jit(solution)/shard_map/ppermute | solution.py:31
  168.7 1.0 copy-start.6
Sparse Core Ops, SparseCore 0:
  209.6 12.6 all-gather.3

commit v2 on v1

v2 whole, which is shorter than its diff:
```python
import functools

import jax
import jax.numpy as jnp
from jax import lax
from jax.experimental import pallas as pl
from jax.experimental.pallas import tpu as pltpu
from jax.sharding import Mesh
from jax.sharding import PartitionSpec as P

D = 8192
STEPS = 3
DH = 128
EPS = 1e-06
LANES = 128
BATCH = ("z", "core")
TENSOR = ("y", "x")
VMEM = pltpu.CompilerParams(vmem_limit_bytes=48 * 1024 * 1024)


def swap_cores(value):
    return lax.ppermute(value, "core", [(0, 1), (1, 0)])


def pass_on(value):
    zs = lax.axis_size("z")
    pairs = []
    for z in range(zs):
        pairs.append((2 * z, 2 * ((z + 1) % zs)))
        pairs.append((2 * z + 1, 2 * ((z - 1) % zs) + 1))
    return lax.ppermute(value, BATCH, pairs)


def pieces_of(sums, source):
    high = lax.reduce_precision(sums, 8, 7)
    middle = lax.reduce_precision(sums - high, 8, 7)
    low = sums - high - middle
    lane = lax.broadcasted_iota(jnp.int32, (sums.shape[0], LANES), 1) - 3 * source
    return jnp.where(lane == 0, high, jnp.where(lane == 1, middle, jnp.where(lane == 2, low, 0.0)))


def product_kernel(chips, first, place_ref, rows_ref, gain_ref, weight_ref, out_ref, picked_ref):
    width = weight_ref.shape[1]
    share = picked_ref.shape[0] // (2 * STEPS * chips)
    zs = rows_ref.shape[1] // (2 * share) if first else rows_ref.shape[0] // 2
    start, source = place_ref[0], place_ref[1]
    for c in range(chips):
        chip = start + c
        chip = jnp.where(chip >= zs, chip - zs, chip)
        for core in range(2):
            for step in range(STEPS):
                at = ((c * 2 + core) * STEPS + step) * share
                if first:
                    from_row = pl.multiple_of(chip * (2 * share) + core * share, share)
                    values = rows_ref[step, pl.ds(from_row, share), :].astype(jnp.float32)
                    picked_ref[at : at + share, :] = (values * gain_ref[...]).astype(jnp.bfloat16)
                else:
                    block = rows_ref[chip * 2 + core, step * share : (step + 1) * share, :]
                    picked_ref[at : at + share, :] = block
                    values = block.astype(jnp.float32) * gain_ref[...]
                squares = jnp.sum(values * values, axis=-1, keepdims=True)
                out_ref[at : at + share, width:] = pieces_of(squares, source).astype(out_ref.dtype)
    chunk = 256
    for at in range(0, width, chunk):
        out_ref[:, at : at + chunk] = jnp.dot(
            picked_ref[...], weight_ref[:, at : at + chunk], preferred_element_type=jnp.float32
        ).astype(out_ref.dtype)


def product(rows, gain, weight, chips, start, source, first, dtype):
    share = (rows.shape[1] // 16) if first else rows.shape[1] // STEPS
    count = chips * 2 * STEPS * share
    depth, width = weight.shape
    place = jnp.stack([start, source]).astype(jnp.int32)
    out = pl.pallas_call(
        functools.partial(product_kernel, chips, first),
        in_specs=[pl.BlockSpec(memory_space=pltpu.SMEM)] + [pl.BlockSpec(memory_space=pltpu.VMEM)] * 3,
        out_specs=pl.BlockSpec(memory_space=pltpu.VMEM),
        out_shape=jax.ShapeDtypeStruct((count, width + LANES), dtype),
        scratch_shapes=[pltpu.VMEM((count, depth), jnp.bfloat16)],
        compiler_params=VMEM,
    )(place, rows, gain[None, :], weight)
    return out.reshape(chips, 2, STEPS * share, width + LANES)


def sum_to_owner(rows, gain, weight, first):
    zs = lax.axis_size("z")
    half = zs // 2
    z, core = lax.axis_index("z"), lax.axis_index("core")
    source = z * 2 + core
    ahead = core == 0
    theirs_from = jnp.where(ahead, z + half, z + 1) % zs
    mine_from = jnp.where(ahead, z, z + half) % zs
    theirs = product(rows, gain, weight, half, theirs_from, source, first, jnp.bfloat16)
    got = swap_cores(theirs)
    mine = product(rows, gain, weight, half + 1, mine_from, source, first, jnp.bfloat16)

    def at(distance):
        in_mine = jnp.where(ahead, distance, half - distance)
        in_got = jnp.where(ahead, distance - 1, half - distance)
        own = lax.dynamic_index_in_dim(mine, in_mine, 0, keepdims=False).astype(jnp.float32)
        other = lax.dynamic_index_in_dim(got, in_got, 0, keepdims=False).astype(jnp.float32)
        return own + other

    carried = lax.dynamic_index_in_dim(at(half), core, 0, keepdims=False).astype(jnp.bfloat16)
    carried = pass_on(carried)
    which = lax.broadcasted_iota(jnp.int32, (2, 1, 1), 0) == core
    total = at(half - 1) + jnp.where(which, carried.astype(jnp.float32)[None], 0.0)
    for distance in range(half - 2, -1, -1):
        carried = pass_on(total.astype(jnp.bfloat16)).astype(jnp.float32)
        if distance > 0:
            total = at(distance) + carried
    own = lax.dynamic_index_in_dim(mine, jnp.where(ahead, 0, half), 0, keepdims=False)
    total = own.astype(jnp.float32) + carried
    away = lax.dynamic_index_in_dim(total, 1 - core, 0, keepdims=False).astype(jnp.bfloat16)
    return lax.dynamic_index_in_dim(total, core, 0, keepdims=False), swap_cores(away)


def attention_kernel(decay_ref, ours_ref, our_sums_ref, theirs_ref, their_sums_ref, state_ref, gain_ref, mask_ref, out_ref):
    head = pl.program_id(0)
    rows = ours_ref.shape[0]
    mine = rows // STEPS
    squares = jnp.sum(our_sums_ref[...] + their_sums_ref[...].astype(jnp.float32), axis=-1, keepdims=True)
    parts = (ours_ref[...] + theirs_ref[...].astype(jnp.float32)) * lax.rsqrt(squares / D + EPS)
    scale = DH ** (-0.5)
    queries = parts[:, :DH] * scale
    keys = parts[:, DH : 2 * DH] * scale
    values = parts[:, 2 * DH :]
    rate = decay_ref[head]
    turned = queries.T
    found = [[] for _ in range(STEPS)]
    for request in range(mine):
        block = state_ref[request, 0]
        for step in range(STEPS):
            at = step * mine + request
            found[step].append(jnp.sum(turned[:, at : at + 1] * block, axis=0, keepdims=True))
    power = rate
    for step in range(STEPS):
        here = slice(step * mine, (step + 1) * mine)
        total = power * jnp.concatenate(found[step], axis=0)
        power = power * rate
        factor = None
        for earlier in range(step, -1, -1):
            there = slice(earlier * mine, (earlier + 1) * mine)
            score = jnp.sum(queries[here] * keys[there], axis=-1, keepdims=True)
            if factor is not None:
                score = score * factor
            total = total + score * values[there]
            factor = rate if factor is None else factor * rate
        total = total * lax.rsqrt(jnp.mean(total * total, axis=-1, keepdims=True) + EPS)
        spiked = total * gain_ref[...] * mask_ref[step].astype(jnp.float32)
        out_ref[here, :] = spiked.astype(jnp.bfloat16)


def attention(decay, ours, theirs, state, head_gain, att_mask):
    rows, width = ours.shape
    mine, heads = state.shape[:2]
    last = width // LANES - 1
    return pl.pallas_call(
        attention_kernel,
        grid=(heads,),
        in_specs=[
            pl.BlockSpec(memory_space=pltpu.SMEM),
            pl.BlockSpec((rows, 3 * DH), lambda h: (0, h)),
            pl.BlockSpec((rows, LANES), lambda h: (0, last)),
            pl.BlockSpec((rows, 3 * DH), lambda h: (0, h)),
            pl.BlockSpec((rows, LANES), lambda h: (0, last)),
            pl.BlockSpec((mine, 1, DH, DH), lambda h: (0, h, 0, 0)),
            pl.BlockSpec((1, DH), lambda h: (0, h)),
            pl.BlockSpec((STEPS, mine, DH), lambda h: (0, 0, h)),
        ],
        out_specs=pl.BlockSpec((rows, DH), lambda h: (0, h)),
        out_shape=jax.ShapeDtypeStruct((rows, heads * DH), jnp.bfloat16),
        compiler_params=VMEM,
    )(decay, ours, ours, theirs, theirs, state, head_gain[None, :], att_mask)


def gathered_product(value, weight):
    zs = lax.axis_size("z")
    half = zs // 2
    z, core = lax.axis_index("z"), lax.axis_index("core")
    towards = jnp.where(core == 0, -1, 1)
    rows, width = value.shape[0], weight.shape[1]
    out = jnp.zeros((zs, 2, rows, width), jnp.bfloat16)

    def multiply(blocks):
        return jnp.dot(blocks.reshape(-1, blocks.shape[-1]), weight, preferred_element_type=jnp.float32).astype(
            jnp.bfloat16
        ).reshape(blocks.shape[:-1] + (width,))

    def put(out, blocks, chip):
        return lax.dynamic_update_slice(out, blocks[None], ((chip + zs) % zs, 0, 0, 0))

    sibling = swap_cores(value)
    low, high = jnp.where(core == 0, value, sibling), jnp.where(core == 0, sibling, value)
    moving = jnp.stack([low, high])
    done = multiply(moving)
    out = put(out, done, z)
    for distance in range(1, half):
        moving = pass_on(moving)
        other = swap_cores(moving)
        done = multiply(jnp.stack([moving, other]))
        out = put(out, done[0], z + towards * distance)
        out = put(out, done[1], z - towards * distance)
    last = pass_on(lax.dynamic_index_in_dim(moving, core, 0, keepdims=False))
    other = swap_cores(last)
    low, high = jnp.where(core == 0, last, other), jnp.where(core == 0, other, last)
    return put(out, multiply(jnp.stack([low, high])), z + half)


def on_device(
    inputs,
    in_gain,
    qkv_weight,
    decay,
    state,
    head_gain,
    out_weight,
    mid_gain,
    up_weight,
    down_weight,
    att_mask,
    ffn_mask,
):
    blocks = lax.axis_size("core") * lax.axis_size("z")
    share = inputs.shape[1] // blocks
    features = inputs.shape[2]
    each = STEPS * share
    ours, theirs = sum_to_owner(inputs, in_gain, qkv_weight, True)
    spiked = attention(decay, ours, theirs, state, head_gain, att_mask)

    everyone = lax.all_gather(spiked, BATCH, axis=0, tiled=True)
    partial = jnp.dot(everyone, out_weight, preferred_element_type=jnp.float32).astype(jnp.bfloat16)
    partial = lax.all_to_all(partial.reshape(blocks, each, features), TENSOR, 0, 0, tiled=True)
    start = lax.axis_index(TENSOR) * share
    kept = lax.dynamic_slice_in_dim(inputs, start, share, 1).reshape(each, features).astype(jnp.float32)
    mixed = kept + jnp.sum(partial.astype(jnp.float32), axis=0)

    hidden = (mixed * mid_gain).astype(jnp.bfloat16)
    hidden = jnp.broadcast_to(hidden[None], (blocks, each, features))
    hidden = lax.all_to_all(hidden, TENSOR, 0, 0, tiled=True)
    ours, theirs = sum_to_owner(hidden, 1.0 / mid_gain, up_weight, False)
    total = ours + theirs.astype(jnp.float32)
    units = up_weight.shape[1]
    inverse = lax.rsqrt(jnp.sum(total[:, units:], axis=-1, keepdims=True) / D + EPS)
    gate = total[:, :units] * inverse
    fired = ffn_mask.reshape(each, units) * (gate / (1.0 + jnp.exp(-gate)))

    partial = gathered_product(fired.astype(jnp.bfloat16), down_weight)
    partial = lax.all_to_all(partial.reshape(blocks, each, features), TENSOR, 0, 0, tiled=True)
    final = mixed + jnp.sum(partial.astype(jnp.float32), axis=0)
    return final.astype(jnp.bfloat16).reshape(STEPS, share, features)


def solution(mesh):
    devices = mesh.devices.reshape(8, 2, 4, 4)
    inner = Mesh(devices, ("z", "core", "y", "x"))
    return jax.shard_map(
        on_device,
        mesh=inner,
        in_specs=(
            P(None, None, BATCH),
            P(BATCH),
            P(BATCH, TENSOR),
            P(TENSOR),
            P(BATCH, TENSOR, None, None),
            P(TENSOR),
            P(TENSOR, BATCH),
            P(BATCH),
            P(BATCH, TENSOR),
            P(TENSOR, BATCH),
            P(None, BATCH, TENSOR),
            P(None, BATCH, TENSOR),
        ),
        out_specs=P(None, TENSOR, BATCH),
        check_vma=False,
    )
```

time: 256 us -> 223 us (0.87); the launches traced: 255 us -> 219 us
  blocking collectives: 176 us -> 36.5 us
  waiting for transfers between devices: 30.2 us -> 86.4 us
  starting transfers between devices: 8.43 us -> 52.9 us
  between operations: 13.7 us -> 0.44 us
  local copies, waits for them, and re-layouts: 3.02 us -> 11.4 us
  other arithmetic: 5.8 us -> 13.5 us
  matrix products: 11.4 us -> 3.85 us
  Pallas kernels: 6.57 us -> 13.7 us
    all_to_all x6 -> x1, blocking collectives: 174 us -> 17.8 us  [on_device(): lax.all_to_all(partial.reshape(blocks, each, features), TENSOR, 0, 0, til...]
    ppermute x0 -> x12, waiting for transfers between devices: none -> 51.6 us  [pass_on(): return lax.ppermute(value, BATCH, pairs)]
    ppermute x0 -> x12, starting transfers between devices: none -> 41.4 us  [pass_on(): return lax.ppermute(value, BATCH, pairs)]
    all_gather x1, blocking collectives: 2.36 us -> 18.8 us  [on_device(): everyone = lax.all_gather(spiked, BATCH, axis=0, tiled=True)]
    all_to_all x1 -> x2, waiting for transfers between devices: 13.1 us -> 27.8 us  [the longest x1 14 us: on_device(): lax.all_to_all(partial.reshape(blocks, each, features), TENSOR, 0, 0, til...]
    all_gather x1 -> x0, waiting for transfers between devices: 12.9 us -> none  [gather_rows(): both = lax.all_gather(along_z, 'core', axis=0, tiled=False)]
    dot_general x5, matrix products: 9.99 us -> 2.4 us  [multiply(): jnp.dot(blocks.reshape(-1, blocks.shape[-1]), weight, preferred_element_t...]
    unnamed x22 -> x34, local copies, waits for them, and re-layouts: 2.3 us -> 9.38 us
  transfers between devices with their start and end apart: 6 -> 23, of which waited for: 5 -> 19; matrix products, arithmetic and copies ran while one was open for 1% -> 2% of each run, Pallas kernels for 0% -> 1%
where the time goes in v2:
time: 223 us; the launch traced here: 219 us
  waiting for transfers between devices  86.4 us (39%)
  starting transfers between devices  52.9 us (24%)
  blocking collectives  36.5 us (16%)
  Pallas kernels  13.7 us (6%)
  other arithmetic  13.5 us (6%)
  local copies, waits for them, and re-layouts  11.4 us (5%)
  matrix products  3.85 us (2%)
    ppermute x12, waiting for transfers between devices, pass_on(): return lax.ppermute(value, BATCH, pairs)  51.6 us
    ppermute x12, starting transfers between devices, pass_on(): return lax.ppermute(value, BATCH, pairs)  41.4 us
    all_gather x1, blocking collectives, on_device(): everyone = lax.all_gather(spiked, BATCH, axis=0, tiled=True)  18.8 us
    all_to_all x1, blocking collectives, on_device(): lax.all_to_all(partial.reshape(blocks, each, features), TENSOR, 0, 0, til...  17.8 us
    all_to_all x1, waiting for transfers between devices, on_device(): lax.all_to_all(partial.reshape(blocks, each, features), TENSOR, 0, 0, til...  14 us
    all_to_all x1, waiting for transfers between devices, on_device(): hidden = lax.all_to_all(hidden, TENSOR, 0, 0, tiled=True)  13.8 us
    unnamed x34, local copies, waits for them, and re-layouts  9.38 us
    all_to_all x1, starting transfers between devices, on_device(): lax.all_to_all(partial.reshape(blocks, each, features), TENSOR, 0, 0, til...  7.16 us
  transfers between devices with their start and end apart: 23, of which 19 were waited for; matrix products, arithmetic and copies ran while one was open for 2% of the time, Pallas kernels for 1%

profile of v2, /device:TPU:96, one launch (start us, length us, event | category | flops | bytes accessed | tf_op | source)
XLA Modules:
  0.0 218.7 jit_solution(2055994656283177120)
XLA Ops:
  20.6 3.7 %collective-permute-start.2 = (bf16[2,48,1664]{2,1,0:T(8,128)(2,1)}, bf16[2,48,1664]{2,1,0:T(8,128)(2,1)}, u32[]{:S(2)}, u32[]{:S(2)}) collective-permute-start(bf16[2,48,1664]{2,1,0:T(8,128)(2,1)} %fusion.6), channel_id=1, source_target_pairs={{0,32},{16,240},{32,64},{48,16},{64,96},{80,48},{96,128},{112,80},... | collective-permute-start | bytes 958472 | tf_op jit(solution)/shard_map/ppermute | solution.py:31
  25.0 4.1 %collective-permute-done.2 = bf16[2,48,1664]{2,1,0:T(8,128)(2,1)} collective-permute-done((bf16[2,48,1664]{2,1,0:T(8,128)(2,1)}, bf16[2,48,1664]{2,1,0:T(8,128)(2,1)}, u32[]{:S(2)}, u32[]{:S(2)}) %collective-permute-start.2) | collective-permute-done | bytes 319520 | tf_op jit(solution)/shard_map/ppermute | solution.py:31
  31.1 3.7 %collective-permute-start.3 = (bf16[2,48,1664]{2,1,0:T(8,128)(2,1)}, bf16[2,48,1664]{2,1,0:T(8,128)(2,1)}, u32[]{:S(2)}, u32[]{:S(2)}) collective-permute-start(bf16[2,48,1664]{2,1,0:T(8,128)(2,1)} %fusion.5), channel_id=1, source_target_pairs={{0,32},{16,240},{32,64},{48,16},{64,96},{80,48},{96,128},{112,80},... | collective-permute-start | bytes 958472 | tf_op jit(solution)/shard_map/ppermute | solution.py:31
  34.8 4.8 %collective-permute-done.3 = bf16[2,48,1664]{2,1,0:T(8,128)(2,1)} collective-permute-done((bf16[2,48,1664]{2,1,0:T(8,128)(2,1)}, bf16[2,48,1664]{2,1,0:T(8,128)(2,1)}, u32[]{:S(2)}, u32[]{:S(2)}) %collective-permute-start.3) | collective-permute-done | bytes 319520 | tf_op jit(solution)/shard_map/ppermute | solution.py:31
  41.6 3.7 %collective-permute-start.4 = (bf16[2,48,1664]{2,1,0:T(8,128)(2,1)}, bf16[2,48,1664]{2,1,0:T(8,128)(2,1)}, u32[]{:S(2)}, u32[]{:S(2)}) collective-permute-start(bf16[2,48,1664]{2,1,0:T(8,128)(2,1)} %fusion.7), channel_id=1, source_target_pairs={{0,32},{16,240},{32,64},{48,16},{64,96},{80,48},{96,128},{112,80},... | collective-permute-start | bytes 958472 | tf_op jit(solution)/shard_map/ppermute | solution.py:31
  45.3 4.8 %collective-permute-done.4 = bf16[2,48,1664]{2,1,0:T(8,128)(2,1)} collective-permute-done((bf16[2,48,1664]{2,1,0:T(8,128)(2,1)}, bf16[2,48,1664]{2,1,0:T(8,128)(2,1)}, u32[]{:S(2)}, u32[]{:S(2)}) %collective-permute-start.4) | collective-permute-done | bytes 319520 | tf_op jit(solution)/shard_map/ppermute | solution.py:31
  54.9 6.6 %shard_map.120 = bf16[48,512]{1,0:T(8,128)(2,1)S(1)} custom-call(f32[4]{0:T(128)S(1)} %copy-done.13, f32[48,1664]{1,0:T(8,128)S(1)} %dynamic-slice_bitcast_fusion.ours_ref.our_sums_ref, f32[48,1664]{1,0:T(8,128)S(1)} %dynamic-slice_bitcast_fusion.ours_ref.our_sums_ref, bf16[48,1664]{1,0:T(8,128)(2,1)S(1)} %collective-permute-done.5.theirs_ref.their_sums_ref, ...), custom_call_target="tpu_custom_call" | custom-call | tf_op jit(solution)/shard_map/pallas_call | solution.py:159
  61.5 18.8 %all_gather.3 = bf16[768,512]{1,0:T(8,128)(2,1)S(1)} all-gather(bf16[48,512]{1,0:T(8,128)(2,1)S(1)} %shard_map.120), channel_id=1, replica_groups=mesh['z'=8,'core'=2,'y'=4,'x'=4] {'z','core'}, dimensions={0}, use_global_device_ids=true | all-gather | bytes 835584 | tf_op jit(solution)/shard_map/all_gather | solution.py:232
  81.7 7.2 %all-to-all-start = ((bf16[16,48,512]{2,1,0:T(8,128)(2,1)}), bf16[16,48,512]{2,1,0:T(8,128)(2,1)S(1)}, u32[]{:S(2)}, u32[]{:S(2)}) async-start(bf16[16,48,512]{2,1,0:T(8,128)(2,1)} %bitcast.15), calls=%async_computation | async-start | bytes 1572864 | tf_op jit(solution)/shard_map/all_to_all | solution.py:234
  89.7 14.0 %all-to-all-done = bf16[16,48,512]{2,1,0:T(8,128)(2,1)S(1)} async-done(((bf16[16,48,512]{2,1,0:T(8,128)(2,1)}), bf16[16,48,512]{2,1,0:T(8,128)(2,1)S(1)}, u32[]{:S(2)}, u32[]{:S(2)}) %all-to-all-start) | async-done | bytes 786464 | tf_op jit(solution)/shard_map/all_to_all | solution.py:234
  108.5 13.8 %all-to-all-done.1.rows_ref = bf16[16,48,512]{2,1,0:T(8,128)(2,1)S(1)} async-done(((bf16[16,48,512]{2,1,0:T(8,128)(2,1)}), bf16[16,48,512]{2,1,0:T(8,128)(2,1)S(1)}, u32[]{:S(2)}, u32[]{:S(2)}) %all-to-all-start.1) | async-done | bytes 786464 | tf_op jit(solution)/shard_map/all_to_all | solution.py:241
  130.5 4.0 %collective-permute-done.7 = bf16[48,1920]{1,0:T(8,128)(2,1)S(1)} collective-permute-done((bf16[48,1920]{1,0:T(8,128)(2,1)S(1)}, bf16[48,1920]{1,0:T(8,128)(2,1)S(1)}, u32[]{:S(2)}, u32[]{:S(2)}) %collective-permute-start.7) | collective-permute-done | bytes 184352 | tf_op jit(solution)/shard_map/ppermute | solution.py:31
  137.5 5.0 %collective-permute-done.8 = bf16[2,48,1920]{2,1,0:T(8,128)(2,1)S(1)} collective-permute-done((bf16[2,48,1920]{2,1,0:T(8,128)(2,1)S(1)}, bf16[2,48,1920]{2,1,0:T(8,128)(2,1)S(1)}, u32[]{:S(2)}, u32[]{:S(2)}) %collective-permute-start.8) | collective-permute-done | bytes 368672 | tf_op jit(solution)/shard_map/ppermute | solution.py:31
  142.7 3.8 %collective-permute-start.9 = (bf16[2,48,1920]{2,1,0:T(8,128)(2,1)S(1)}, bf16[2,48,1920]{2,1,0:T(8,128)(2,1)S(1)}, u32[]{:S(2)}, u32[]{:S(2)}) collective-permute-start(bf16[2,48,1920]{2,1,0:T(8,128)(2,1)S(1)} %fusion.1), channel_id=1, source_target_pairs={{0,32},{16,240},{32,64},{48,16},{64,96},{80,48},{96,128},{112,80},... | collective-permute-start | bytes 1105928 | tf_op jit(solution)/shard_map/ppermute | solution.py:31
  146.4 5.0 %collective-permute-done.9 = bf16[2,48,1920]{2,1,0:T(8,128)(2,1)S(1)} collective-permute-done((bf16[2,48,1920]{2,1,0:T(8,128)(2,1)S(1)}, bf16[2,48,1920]{2,1,0:T(8,128)(2,1)S(1)}, u32[]{:S(2)}, u32[]{:S(2)}) %collective-permute-start.9) | collective-permute-done | bytes 368672 | tf_op jit(solution)/shard_map/ppermute | solution.py:31
  151.6 3.8 %collective-permute-start.10 = (bf16[2,48,1920]{2,1,0:T(8,128)(2,1)S(1)}, bf16[2,48,1920]{2,1,0:T(8,128)(2,1)S(1)}, u32[]{:S(2)}, u32[]{:S(2)}) collective-permute-start(bf16[2,48,1920]{2,1,0:T(8,128)(2,1)S(1)} %fusion.3), channel_id=1, source_target_pairs={{0,32},{16,240},{32,64},{48,16},{64,96},{80,48},{96,128},{112,80},... | collective-permute-start | bytes 1105928 | tf_op jit(solution)/shard_map/ppermute | solution.py:31
  155.4 5.0 %collective-permute-done.10 = bf16[2,48,1920]{2,1,0:T(8,128)(2,1)S(1)} collective-permute-done((bf16[2,48,1920]{2,1,0:T(8,128)(2,1)S(1)}, bf16[2,48,1920]{2,1,0:T(8,128)(2,1)S(1)}, u32[]{:S(2)}, u32[]{:S(2)}) %collective-permute-start.10) | collective-permute-done | bytes 368672 | tf_op jit(solution)/shard_map/ppermute | solution.py:31
  164.0 3.8 %collective-permute-start.13 = (bf16[2,48,1792]{2,1,0:T(8,128)(2,1)S(1)}, bf16[2,48,1792]{2,1,0:T(8,128)(2,1)S(1)}, u32[]{:S(2)}, u32[]{:S(2)}) collective-permute-start(bf16[2,48,1792]{2,1,0:T(8,128)(2,1)S(1)} %pad_maximum_fusion.3), channel_id=1, source_target_pairs={{0,32},{16,240},{32,64},{48,16},{64,96},{80,48},{96,128},{112,80},... | collective-permute-start | bytes 1032200 | tf_op jit(solution)/shard_map/ppermute | solution.py:31
  167.7 4.8 %collective-permute-done.13 = bf16[2,48,1792]{2,1,0:T(8,128)(2,1)S(1)} collective-permute-done((bf16[2,48,1792]{2,1,0:T(8,128)(2,1)S(1)}, bf16[2,48,1792]{2,1,0:T(8,128)(2,1)S(1)}, u32[]{:S(2)}, u32[]{:S(2)}) %collective-permute-start.13) | collective-permute-done | bytes 344096 | tf_op jit(solution)/shard_map/ppermute | solution.py:31
  173.0 3.8 %collective-permute-start.15 = (bf16[2,48,1792]{2,1,0:T(8,128)(2,1)S(1)}, bf16[2,48,1792]{2,1,0:T(8,128)(2,1)S(1)}, u32[]{:S(2)}, u32[]{:S(2)}) collective-permute-start(bf16[2,48,1792]{2,1,0:T(8,128)(2,1)S(1)} %collective-permute-done.13), channel_id=1, source_target_pairs={{0,32},{16,240},{32,64},{48,16},{64,96},{80,48},{96,128},{112,80},... | collective-permute-start | bytes 1032200 | tf_op jit(solution)/shard_map/ppermute | solution.py:31
  177.4 4.2 %collective-permute-done.15 = bf16[2,48,1792]{2,1,0:T(8,128)(2,1)S(1)} collective-permute-done((bf16[2,48,1792]{2,1,0:T(8,128)(2,1)S(1)}, bf16[2,48,1792]{2,1,0:T(8,128)(2,1)S(1)}, u32[]{:S(2)}, u32[]{:S(2)}) %collective-permute-start.15) | collective-permute-done | bytes 344096 | tf_op jit(solution)/shard_map/ppermute | solution.py:31
  185.4 4.6 %collective-permute-done.17 = bf16[2,48,1792]{2,1,0:T(8,128)(2,1)S(1)} collective-permute-done((bf16[2,48,1792]{2,1,0:T(8,128)(2,1)S(1)}, bf16[2,48,1792]{2,1,0:T(8,128)(2,1)S(1)}, u32[]{:S(2)}, u32[]{:S(2)}) %collective-permute-start.17) | collective-permute-done | bytes 344096 | tf_op jit(solution)/shard_map/ppermute | solution.py:31
  190.1 3.8 %collective-permute-start.19 = (bf16[48,1792]{1,0:T(8,128)(2,1)S(1)}, bf16[48,1792]{1,0:T(8,128)(2,1)S(1)}, u32[]{:S(2)}, u32[]{:S(2)}) collective-permute-start(bf16[48,1792]{1,0:T(8,128)(2,1)S(1)} %dynamic-slice_bitcast_fusion.1), channel_id=1, source_target_pairs={{0,32},{16,240},{32,64},{48,16},{64,96},{80,48},{96,128},{112,80},... | collective-permute-start | bytes 516104 | tf_op jit(solution)/shard_map/ppermute | solution.py:31
  199.4 17.8 %all_to_all.15 = bf16[16,48,512]{2,1,0:T(8,128)(2,1)S(1)} all-to-all(bf16[16,48,512]{2,1,0:T(8,128)(2,1)S(1)} %bitcast.123), channel_id=1, replica_groups=mesh['z'=8,'core'=2,'y'=4,'x'=4] {'y','x'}, dimensions={0} | all-to-all | bytes 1572864 | tf_op jit(solution)/shard_map/all_to_all | solution.py:250
  (119 shorter events, 63.9 us)
Async XLA Ops:
  0.0 172.5 %copy-start = (bf16[1792,512]{1,0:T(8,128)(2,1)S(1)}, bf16[1792,512]{1,0:T(8,128)(2,1)}, u32[]{:S(2)}) copy-start(bf16[1792,512]{1,0:T(8,128)(2,1)} %param.21) | copy-start | bytes 5505028
  5.8 3.9 %collective-permute-start = (bf16[4,2,48,1664]{3,2,1,0:T(8,128)(2,1)}, bf16[4,2,48,1664]{3,2,1,0:T(8,128)(2,1)}, u32[]{:S(2)}, u32[]{:S(2)}) collective-permute-start(bf16[4,2,48,1664]{3,2,1,0:T(8,128)(2,1)} %bitcast.6), channel_id=1, source_target_pairs={{0,16},{16,0},{1,17},{17,1},{2,18},{18,2},{3,19},{19,3},{4,20},{20... | collective-permute-start | bytes 3833864 | tf_op jit(solution)/shard_map/ppermute | solution.py:22
  11.5 6.2 %collective-permute-start.1 = (bf16[48,1664]{1,0:T(8,128)(2,1)}, bf16[48,1664]{1,0:T(8,128)(2,1)}, u32[]{:S(2)}, u32[]{:S(2)}) collective-permute-start(bf16[48,1664]{1,0:T(8,128)(2,1)} %fusion.11), channel_id=1, source_target_pairs={{0,32},{16,240},{32,64},{48,16},{64,96},{80,48},{96,128},{112,80},... | collective-permute-start | bytes 479240 | tf_op jit(solution)/shard_map/ppermute | solution.py:31
  20.6 8.5 %collective-permute-start.2 = (bf16[2,48,1664]{2,1,0:T(8,128)(2,1)}, bf16[2,48,1664]{2,1,0:T(8,128)(2,1)}, u32[]{:S(2)}, u32[]{:S(2)}) collective-permute-start(bf16[2,48,1664]{2,1,0:T(8,128)(2,1)} %fusion.6), channel_id=1, source_target_pairs={{0,32},{16,240},{32,64},{48,16},{64,96},{80,48},{96,128},{112,80},... | collective-permute-start | bytes 958472 | tf_op jit(solution)/shard_map/ppermute | solution.py:31
  31.1 8.5 %collective-permute-start.3 = (bf16[2,48,1664]{2,1,0:T(8,128)(2,1)}, bf16[2,48,1664]{2,1,0:T(8,128)(2,1)}, u32[]{:S(2)}, u32[]{:S(2)}) collective-permute-start(bf16[2,48,1664]{2,1,0:T(8,128)(2,1)} %fusion.5), channel_id=1, source_target_pairs={{0,32},{16,240},{32,64},{48,16},{64,96},{80,48},{96,128},{112,80},... | collective-permute-start | bytes 958472 | tf_op jit(solution)/shard_map/ppermute | solution.py:31
  41.6 8.5 %collective-permute-start.4 = (bf16[2,48,1664]{2,1,0:T(8,128)(2,1)}, bf16[2,48,1664]{2,1,0:T(8,128)(2,1)}, u32[]{:S(2)}, u32[]{:S(2)}) collective-permute-start(bf16[2,48,1664]{2,1,0:T(8,128)(2,1)} %fusion.7), channel_id=1, source_target_pairs={{0,32},{16,240},{32,64},{48,16},{64,96},{80,48},{96,128},{112,80},... | collective-permute-start | bytes 958472 | tf_op jit(solution)/shard_map/ppermute | solution.py:31
  51.2 1.5 collective-permute-start.5
  81.7 22.0 %all-to-all-start = ((bf16[16,48,512]{2,1,0:T(8,128)(2,1)}), bf16[16,48,512]{2,1,0:T(8,128)(2,1)S(1)}, u32[]{:S(2)}, u32[]{:S(2)}) async-start(bf16[16,48,512]{2,1,0:T(8,128)(2,1)} %bitcast.15), calls=%async_computation | async-start | bytes 1572864 | tf_op jit(solution)/shard_map/all_to_all | solution.py:234
  104.8 17.4 %all-to-all-start.1 = ((bf16[16,48,512]{2,1,0:T(8,128)(2,1)}), bf16[16,48,512]{2,1,0:T(8,128)(2,1)S(1)}, u32[]{:S(2)}, u32[]{:S(2)}) async-start(bf16[16,48,512]{2,1,0:T(8,128)(2,1)} %broadcast_in_dim.70), calls=%async_computation.1 | async-start | bytes 1572864 | tf_op jit(solution)/shard_map/all_to_all | solution.py:241
  125.2 3.4 %collective-permute-start.6 = (bf16[4,2,48,1920]{3,2,1,0:T(8,128)(2,1)S(1)}, bf16[4,2,48,1920]{3,2,1,0:T(8,128)(2,1)S(1)}, u32[]{:S(2)}, u32[]{:S(2)}) collective-permute-start(bf16[4,2,48,1920]{3,2,1,0:T(8,128)(2,1)S(1)} %bitcast.117), channel_id=1, source_target_pairs={{0,16},{16,0},{1,17},{17,1},{2,18},{18,2},{3,19},{19,3},{4,20},{20... | collective-permute-start | bytes 4423688 | tf_op jit(solution)/shard_map/ppermute | solution.py:22
  128.6 5.8 %collective-permute-start.7 = (bf16[48,1920]{1,0:T(8,128)(2,1)S(1)}, bf16[48,1920]{1,0:T(8,128)(2,1)S(1)}, u32[]{:S(2)}, u32[]{:S(2)}) collective-permute-start(bf16[48,1920]{1,0:T(8,128)(2,1)S(1)} %fusion.9), channel_id=1, source_target_pairs={{0,32},{16,240},{32,64},{48,16},{64,96},{80,48},{96,128},{112,80},... | collective-permute-start | bytes 552968 | tf_op jit(solution)/shard_map/ppermute | solution.py:31
  134.6 7.9 %collective-permute-start.8 = (bf16[2,48,1920]{2,1,0:T(8,128)(2,1)S(1)}, bf16[2,48,1920]{2,1,0:T(8,128)(2,1)S(1)}, u32[]{:S(2)}, u32[]{:S(2)}) collective-permute-start(bf16[2,48,1920]{2,1,0:T(8,128)(2,1)S(1)} %fusion.2), channel_id=1, source_target_pairs={{0,32},{16,240},{32,64},{48,16},{64,96},{80,48},{96,128},{112,80},... | collective-permute-start | bytes 1105928 | tf_op jit(solution)/shard_map/ppermute | solution.py:31
  142.7 8.8 %collective-permute-start.9 = (bf16[2,48,1920]{2,1,0:T(8,128)(2,1)S(1)}, bf16[2,48,1920]{2,1,0:T(8,128)(2,1)S(1)}, u32[]{:S(2)}, u32[]{:S(2)}) collective-permute-start(bf16[2,48,1920]{2,1,0:T(8,128)(2,1)S(1)} %fusion.1), channel_id=1, source_target_pairs={{0,32},{16,240},{32,64},{48,16},{64,96},{80,48},{96,128},{112,80},... | collective-permute-start | bytes 1105928 | tf_op jit(solution)/shard_map/ppermute | solution.py:31
  151.6 8.8 %collective-permute-start.10 = (bf16[2,48,1920]{2,1,0:T(8,128)(2,1)S(1)}, bf16[2,48,1920]{2,1,0:T(8,128)(2,1)S(1)}, u32[]{:S(2)}, u32[]{:S(2)}) collective-permute-start(bf16[2,48,1920]{2,1,0:T(8,128)(2,1)S(1)} %fusion.3), channel_id=1, source_target_pairs={{0,32},{16,240},{32,64},{48,16},{64,96},{80,48},{96,128},{112,80},... | collective-permute-start | bytes 1105928 | tf_op jit(solution)/shard_map/ppermute | solution.py:31
  160.5 1.5 collective-permute-start.11
  162.4 1.5 collective-permute-start.12
  164.0 8.5 %collective-permute-start.13 = (bf16[2,48,1792]{2,1,0:T(8,128)(2,1)S(1)}, bf16[2,48,1792]{2,1,0:T(8,128)(2,1)S(1)}, u32[]{:S(2)}, u32[]{:S(2)}) collective-permute-start(bf16[2,48,1792]{2,1,0:T(8,128)(2,1)S(1)} %pad_maximum_fusion.3), channel_id=1, source_target_pairs={{0,32},{16,240},{32,64},{48,16},{64,96},{80,48},{96,128},{112,80},... | collective-permute-start | bytes 1032200 | tf_op jit(solution)/shard_map/ppermute | solution.py:31
  172.5 4.3 %collective-permute-start.14 = (bf16[2,48,1792]{2,1,0:T(8,128)(2,1)S(1)}, bf16[2,48,1792]{2,1,0:T(8,128)(2,1)S(1)}, u32[]{:S(2)}, u32[]{:S(2)}) collective-permute-start(bf16[2,48,1792]{2,1,0:T(8,128)(2,1)S(1)} %collective-permute-done.13), channel_id=1, source_target_pairs={{0,16},{16,0},{1,17},{17,1},{2,18},{18,2},{3,19},{19,3},{4,20},{20... | collective-permute-start | bytes 1032200 | tf_op jit(solution)/shard_map/ppermute | solution.py:22
  173.0 8.5 %collective-permute-start.15 = (bf16[2,48,1792]{2,1,0:T(8,128)(2,1)S(1)}, bf16[2,48,1792]{2,1,0:T(8,128)(2,1)S(1)}, u32[]{:S(2)}, u32[]{:S(2)}) collective-permute-start(bf16[2,48,1792]{2,1,0:T(8,128)(2,1)S(1)} %collective-permute-done.13), channel_id=1, source_target_pairs={{0,32},{16,240},{32,64},{48,16},{64,96},{80,48},{96,128},{112,80},... | collective-permute-start | bytes 1032200 | tf_op jit(solution)/shard_map/ppermute | solution.py:31
  181.6 8.5 %collective-permute-start.17 = (bf16[2,48,1792]{2,1,0:T(8,128)(2,1)S(1)}, bf16[2,48,1792]{2,1,0:T(8,128)(2,1)S(1)}, u32[]{:S(2)}, u32[]{:S(2)}) collective-permute-start(bf16[2,48,1792]{2,1,0:T(8,128)(2,1)S(1)} %collective-permute-done.15), channel_id=1, source_target_pairs={{0,32},{16,240},{32,64},{48,16},{64,96},{80,48},{96,128},{112,80},... | collective-permute-start | bytes 1032200 | tf_op jit(solution)/shard_map/ppermute | solution.py:31
  185.3 8.5 %collective-permute-start.16 = (bf16[2,48,1792]{2,1,0:T(8,128)(2,1)S(1)}, bf16[2,48,1792]{2,1,0:T(8,128)(2,1)S(1)}, u32[]{:S(2)}, u32[]{:S(2)}) collective-permute-start(bf16[2,48,1792]{2,1,0:T(8,128)(2,1)S(1)} %collective-permute-done.15), channel_id=1, source_target_pairs={{0,16},{16,0},{1,17},{17,1},{2,18},{18,2},{3,19},{19,3},{4,20},{20... | collective-permute-start | bytes 1032200 | tf_op jit(solution)/shard_map/ppermute | solution.py:22
  190.1 6.7 %collective-permute-start.19 = (bf16[48,1792]{1,0:T(8,128)(2,1)S(1)}, bf16[48,1792]{1,0:T(8,128)(2,1)S(1)}, u32[]{:S(2)}, u32[]{:S(2)}) collective-permute-start(bf16[48,1792]{1,0:T(8,128)(2,1)S(1)} %dynamic-slice_bitcast_fusion.1), channel_id=1, source_target_pairs={{0,32},{16,240},{32,64},{48,16},{64,96},{80,48},{96,128},{112,80},... | collective-permute-start | bytes 516104 | tf_op jit(solution)/shard_map/ppermute | solution.py:31
  194.4 4.2 %collective-permute-start.18 = (bf16[2,48,1792]{2,1,0:T(8,128)(2,1)S(1)}, bf16[2,48,1792]{2,1,0:T(8,128)(2,1)S(1)}, u32[]{:S(2)}, u32[]{:S(2)}) collective-permute-start(bf16[2,48,1792]{2,1,0:T(8,128)(2,1)S(1)} %collective-permute-done.17), channel_id=1, source_target_pairs={{0,16},{16,0},{1,17},{17,1},{2,18},{18,2},{3,19},{19,3},{4,20},{20... | collective-permute-start | bytes 1032200 | tf_op jit(solution)/shard_map/ppermute | solution.py:22
  196.8 1.4 collective-permute-start.20
  (16 other events, 163.9 us)
